TPU v7x, 32 devices: a whole 2x2x4 slice. The times are simulated.
32 devices in a mesh: groups: 2 (over x), seq: 16 (over z, y, core).
Axes of the slice: x: 2, y: 2, z: 4, core: 2. Of those that a mesh axis runs over, the one named last changes fastest.
Arguments:
- query: bfloat16 [4096, 1024], P(('groups', 'seq')), parts along dimension 0, may hold values from -6 to 6
- key: bfloat16 [4096, 1024], P(('groups', 'seq')), parts along dimension 0, may hold values from -6 to 6
- value: bfloat16 [4096, 1024], P(('groups', 'seq')), parts along dimension 0, may hold values from -6 to 6
- out_grad: bfloat16 [4096, 1024], P(('groups', 'seq')), parts along dimension 0, may hold values from -6 to 6
- session: int32 [4096], P('groups'), parts along dimension 0, may hold values from 0 to 7, never falling along the last dimension, each value on 1 to 512 neighbouring positions
Outputs:
- attended: bfloat16 [4096, 1024], P(('groups', 'seq')), parts along dimension 0
- query_grad: bfloat16 [4096, 1024], P(('groups', 'seq')), parts along dimension 0
- key_grad: bfloat16 [4096, 1024], P(('groups', 'seq')), parts along dimension 0
- value_grad: bfloat16 [4096, 1024], P(('groups', 'seq')), parts along dimension 0
There are 2 independent parts, one for each index of `groups`. A program takes and returns all parts, laid end to end along the dimension named above; each array names one. Nothing has to cross between parts.
Inputs may be any that keep to these rules, and one draw needn't show every extreme that they name: session ids never fall along the packed order; each session holds 1 to 512 frames and one holds exactly 512.
All inputs are finite; a program needn't handle non-finite values.
Results may differ from a plain program's by a relative error of at most 0.023.
Values may be sent and summed in bfloat16 or wider, within the bound.
A program may use at most 64 MiB of HBM per device.

v0:
```python
import jax
import jax.numpy as jnp
from jax import lax
from jax.sharding import PartitionSpec as P

HEADS = 8
HEAD = 128
REACH = 4


def passed_along(value, axis, steps):
    count = lax.axis_size(axis)
    leading, last = (max(0, -steps), min(count, count - steps))
    return lax.ppermute(value, axis, [(source, source + steps) for source in range(leading, last)])


def by_heads(matrix, head_count):
    return matrix.reshape(matrix.shape[0], head_count, matrix.shape[1] // head_count)


def shards(query, key, value, out_grad, session):
    row_count, features = query.shape
    head_count = HEADS
    scaling = HEAD ** (-0.5)
    width = 2 * REACH + 1
    offset = lax.axis_index("seq") * row_count
    filler = jnp.full((REACH * row_count,), -1, jnp.int32)
    session_padded = jnp.concatenate([filler, session, filler])
    own_session = lax.dynamic_slice_in_dim(session, offset, row_count, 0)
    near_session = lax.dynamic_slice_in_dim(session_padded, offset, width * row_count, 0)
    key_value = jnp.stack((key, value))
    lower_blocks = []
    upper_blocks = []
    for distance in range(1, REACH + 1):
        lower_blocks.append(passed_along(key_value, "seq", distance))
        upper_blocks.append(passed_along(key_value, "seq", -distance))
    blocks = lower_blocks[::-1] + [key_value] + upper_blocks
    masks = []
    for index in range(width):
        block_session = near_session[index * row_count : (index + 1) * row_count]
        masks.append((own_session[:, None] == block_session[None, :])[None])
    query_heads = by_heads(query, head_count)
    grad_heads = by_heads(out_grad, head_count)

    def block_scores(index):
        raw = (
            jnp.einsum(
                "qhd,khd->hqk",
                query_heads,
                by_heads(blocks[index][0], head_count),
                preferred_element_type=jnp.float32,
            )
            * scaling
        )
        return jnp.where(masks[index], raw, -jnp.inf)

    highest = jnp.full((head_count, row_count, 1), -1e30, jnp.float32)
    total = jnp.zeros((head_count, row_count, 1), jnp.float32)
    for index in range(width):
        scores = block_scores(index)
        new_high = jnp.maximum(highest, jnp.max(scores, axis=2, keepdims=True))
        total = total * jnp.exp(highest - new_high) + jnp.sum(
            jnp.exp(scores - new_high), axis=2, keepdims=True
        )
        highest = new_high
    log_total = highest + jnp.log(total)

    def scores_of(index):
        return block_scores(index)

    attended_sum = jnp.zeros((row_count, head_count, features // head_count), jnp.float32)
    for index in range(width):
        probs = jnp.exp(scores_of(index) - log_total).astype(jnp.bfloat16)
        attended_sum = attended_sum + jnp.einsum(
            "hqk,khd->qhd",
            probs,
            by_heads(blocks[index][1], head_count),
            preferred_element_type=jnp.float32,
        )
    attended = attended_sum.reshape(row_count, features).astype(jnp.bfloat16)
    delta = jnp.einsum(
        "qhd,qhd->hq",
        grad_heads,
        by_heads(attended, head_count),
        preferred_element_type=jnp.float32,
    )[:, :, None]
    query_sum = jnp.zeros((row_count, head_count, features // head_count), jnp.float32)
    parts = []
    for index in range(width):
        weights = jnp.exp(scores_of(index) - log_total)
        block_keys = by_heads(blocks[index][0], head_count)
        block_values = by_heads(blocks[index][1], head_count)
        grad_probs = jnp.einsum(
            "qhd,khd->hqk", grad_heads, block_values, preferred_element_type=jnp.float32
        )
        grad_scores = (weights * (grad_probs - delta) * scaling).astype(jnp.bfloat16)
        query_sum = query_sum + jnp.einsum(
            "hqk,khd->qhd", grad_scores, block_keys, preferred_element_type=jnp.float32
        )
        key_part = jnp.einsum(
            "hqk,qhd->khd", grad_scores, query_heads, preferred_element_type=jnp.float32
        )
        value_part = jnp.einsum(
            "hqk,qhd->khd",
            weights.astype(jnp.bfloat16),
            grad_heads,
            preferred_element_type=jnp.float32,
        )
        parts.append(
            jnp.stack(
                (key_part.reshape(row_count, features), value_part.reshape(row_count, features))
            )
        )
    query_grad = query_sum.reshape(row_count, features).astype(jnp.bfloat16)
    gradient_total = parts[REACH]
    carried_down = jnp.zeros_like(gradient_total)
    carried_up = jnp.zeros_like(gradient_total)
    for distance in range(REACH, 0, -1):
        carried_down = passed_along(carried_down + parts[REACH - distance], "seq", -1)
        carried_up = passed_along(carried_up + parts[REACH + distance], "seq", 1)
    gradient_total = gradient_total + carried_down + carried_up
    return (
        attended,
        query_grad,
        gradient_total[0].astype(jnp.bfloat16),
        gradient_total[1].astype(jnp.bfloat16),
    )


def solution(mesh):
    return jax.shard_map(
        shards,
        mesh=mesh,
        in_specs=(
            P(("groups", "seq"), None),
            P(("groups", "seq"), None),
            P(("groups", "seq"), None),
            P(("groups", "seq"), None),
            P("groups"),
        ),
        out_specs=(
            P(("groups", "seq"), None),
            P(("groups", "seq"), None),
            P(("groups", "seq"), None),
            P(("groups", "seq"), None),
        ),
        check_vma=False,
    )
```

profile of v0, /device:TPU:17, one launch (start us, length us, event | category | flops | bytes accessed | tf_op | source)
XLA Modules:
  0.0 217.2 jit_solution(8356552390800106640)
XLA Ops:
  0.6 1.2 copy.138
  2.9 3.3 %collective-permute-start = (bf16[2,128,1024]{1,2,0:T(8,128)(2,1)}, bf16[2,128,1024]{1,2,0:T(8,128)(2,1)}, u32[]{:S(2)}, u32[]{:S(2)}) collective-permute-start(bf16[2,128,1024]{1,2,0:T(8,128)(2,1)} %pad_maximum_fusion.2), channel_id=1, source_target_pairs={{0,4},{1,5},{2,6},{3,7},{4,8},{5,9},{6,10},{7,11},{8,12},{9,13},{1... | collective-permute-start | bytes 1572872 | tf_op jit(solution)/shard_map/ppermute | solution.py:14
  6.2 3.9 %collective-permute-start.6 = (bf16[2,128,1024]{1,2,0:T(8,128)(2,1)}, bf16[2,128,1024]{1,2,0:T(8,128)(2,1)S(1)}, u32[]{:S(2)}, u32[]{:S(2)}) collective-permute-start(bf16[2,128,1024]{1,2,0:T(8,128)(2,1)} %pad_maximum_fusion.2), channel_id=1, source_target_pairs={{3,0},{4,1},{5,2},{6,3},{7,4},{8,5},{9,6},{10,7},{11,8},{12,9},{13... | collective-permute-start | bytes 1572872 | tf_op jit(solution)/shard_map/ppermute | solution.py:14
  10.1 2.1 collective-permute-start.5
  12.2 2.5 %collective-permute-start.4 = (bf16[2,128,1024]{1,2,0:T(8,128)(2,1)}, bf16[2,128,1024]{1,2,0:T(8,128)(2,1)S(1)}, u32[]{:S(2)}, u32[]{:S(2)}) collective-permute-start(bf16[2,128,1024]{1,2,0:T(8,128)(2,1)} %pad_maximum_fusion.2), channel_id=1, source_target_pairs={{1,0},{2,1},{3,2},{4,3},{5,4},{6,5},{7,6},{8,7},{9,8},{10,9},{11,1... | collective-permute-start | bytes 1572872 | tf_op jit(solution)/shard_map/ppermute | solution.py:14
  14.7 3.1 %collective-permute-start.3 = (bf16[2,128,1024]{1,2,0:T(8,128)(2,1)}, bf16[2,128,1024]{1,2,0:T(8,128)(2,1)S(1)}, u32[]{:S(2)}, u32[]{:S(2)}) collective-permute-start(bf16[2,128,1024]{1,2,0:T(8,128)(2,1)} %pad_maximum_fusion.2), channel_id=1, source_target_pairs={{0,1},{1,2},{2,3},{3,4},{4,5},{5,6},{6,7},{7,8},{8,9},{9,10},{10,1... | collective-permute-start | bytes 1572872 | tf_op jit(solution)/shard_map/ppermute | solution.py:14
  19.7 4.0 %collective-permute-start.2 = (bf16[2,128,1024]{1,2,0:T(8,128)(2,1)}, bf16[2,128,1024]{1,2,0:T(8,128)(2,1)S(1)}, u32[]{:S(2)}, u32[]{:S(2)}) collective-permute-start(bf16[2,128,1024]{1,2,0:T(8,128)(2,1)} %pad_maximum_fusion.2), channel_id=1, source_target_pairs={{0,2},{1,3},{2,4},{3,5},{4,6},{5,7},{6,8},{7,9},{8,10},{9,11},{10,... | collective-permute-start | bytes 1572872 | tf_op jit(solution)/shard_map/ppermute | solution.py:14
  25.7 2.3 %collective-permute-start.1 = (bf16[2,128,1024]{1,2,0:T(8,128)(2,1)}, bf16[2,128,1024]{1,2,0:T(8,128)(2,1)S(1)}, u32[]{:S(2)}, u32[]{:S(2)}) collective-permute-start(bf16[2,128,1024]{1,2,0:T(8,128)(2,1)} %pad_maximum_fusion.2), channel_id=1, source_target_pairs={{0,3},{1,4},{2,5},{3,6},{4,7},{5,8},{6,9},{7,10},{8,11},{9,12},{10... | collective-permute-start | bytes 1572872 | tf_op jit(solution)/shard_map/ppermute | solution.py:14
  29.1 25.1 %collective-permute-done.5 = bf16[2,128,1024]{1,2,0:T(8,128)(2,1)} collective-permute-done((bf16[2,128,1024]{1,2,0:T(8,128)(2,1)}, bf16[2,128,1024]{1,2,0:T(8,128)(2,1)}, u32[]{:S(2)}, u32[]{:S(2)}) %collective-permute-start.5) | collective-permute-done | bytes 524320 | tf_op jit(solution)/shard_map/ppermute | solution.py:14
  54.2 1.9 collective-permute-start.7
  60.7 3.6 %collective-permute-done.7 = bf16[2,128,1024]{1,2,0:T(8,128)(2,1)S(1)} collective-permute-done((bf16[2,128,1024]{1,2,0:T(8,128)(2,1)}, bf16[2,128,1024]{1,2,0:T(8,128)(2,1)S(1)}, u32[]{:S(2)}, u32[]{:S(2)}) %collective-permute-start.7) | collective-permute-done | bytes 524320 | tf_op jit(solution)/shard_map/ppermute | solution.py:14
  68.7 1.1 bitcast_convert_fusion
  69.9 2.0 copy.284
  71.9 1.3 multiply_reduce_fusion
  73.3 2.3 %fusion.112 = f32[8,128,128]{1,2,0:T(8,128)} fusion(bf16[128,8,128]{0,2,1:T(8,128)(2,1)S(1)} %copy.208, f32[8,128,128]{1,2,0:T(8,128)} %copy-done.6, f32[8,128]{1,0:T(8,128)S(1)} %log_add_fusion), kind=kOutput, calls=%fused_computation.158 | convolution fusion | flops 33816576 | bytes 1314816 | tf_op jit(solution)/shard_map/hqk,qhd->khd/dot_general | solution.py:103
  77.0 1.2 fusion.108
  78.4 1.1 fusion.104
  81.0 1.1 fusion.85
  82.4 1.2 fusion.88
  90.4 2.1 copy.215
  93.5 2.4 %pad_maximum_fusion = f32[2,128,1024]{2,1,0:T(8,128)} fusion(f32[1,128,1024]{2,1,0:T(8,128)} %copy.216, f32[1,128,1024]{2,1,0:T(8,128)} %copy.215), kind=kLoop, calls=%fused_computation.103 | loop fusion | flops 262144 | bytes 2097152 | tf_op jit(solution)/shard_map/stack | solution.py:110
  95.9 2.1 collective-permute-start.8
  100.2 2.1 copy.239
  103.3 2.3 %pad_maximum_fusion.1 = f32[2,128,1024]{2,1,0:T(8,128)} fusion(f32[1,128,1024]{2,1,0:T(8,128)} %copy.240, f32[1,128,1024]{2,1,0:T(8,128)} %copy.239), kind=kLoop, calls=%fused_computation.107 | loop fusion | flops 262144 | bytes 2097152 | tf_op jit(solution)/shard_map/stack | solution.py:110
  105.6 3.5 %collective-permute-start.12 = (f32[2,128,1024]{2,1,0:T(8,128)}, f32[2,128,1024]{2,1,0:T(8,128)}, u32[]{:S(2)}, u32[]{:S(2)}) collective-permute-start(f32[2,128,1024]{2,1,0:T(8,128)} %pad_maximum_fusion.1), channel_id=1, source_target_pairs={{0,1},{1,2},{2,3},{3,4},{4,5},{5,6},{6,7},{7,8},{8,9},{9,10},{10,1... | collective-permute-start | bytes 3145736 | tf_op jit(solution)/shard_map/ppermute | solution.py:14
  111.2 2.1 copy.221
  114.3 2.1 copy.227
  117.5 2.1 copy.245
  120.6 2.1 copy.251
  122.7 2.1 copy.252
  127.5 1.4 maximum_add_fusion.1
  128.9 1.9 collective-permute-start.9
  130.9 1.4 maximum_add_fusion.4
  132.2 3.6 %collective-permute-start.13 = (f32[2,128,1024]{2,1,0:T(8,128)S(1)}, f32[2,128,1024]{2,1,0:T(8,128)S(1)}, u32[]{:S(2)}, u32[]{:S(2)}) collective-permute-start(f32[2,128,1024]{2,1,0:T(8,128)S(1)} %maximum_add_fusion.4), channel_id=1, source_target_pairs={{0,1},{1,2},{2,3},{3,4},{4,5},{5,6},{6,7},{7,8},{8,9},{9,10},{10,1... | collective-permute-start | bytes 3145736 | tf_op jit(solution)/shard_map/ppermute | solution.py:14
  135.9 1.1 fusion.94
  138.3 17.9 %collective-permute-done.9 = f32[2,128,1024]{2,1,0:T(8,128)S(1)} collective-permute-done((f32[2,128,1024]{2,1,0:T(8,128)S(1)}, f32[2,128,1024]{2,1,0:T(8,128)S(1)}, u32[]{:S(2)}, u32[]{:S(2)}) %collective-permute-start.9) | collective-permute-done | bytes 1048608 | tf_op jit(solution)/shard_map/ppermute | solution.py:14
  156.3 1.1 maximum_add_fusion.2
  157.4 1.9 collective-permute-start.10
  159.3 7.5 %collective-permute-done.13 = f32[2,128,1024]{2,1,0:T(8,128)S(1)} collective-permute-done((f32[2,128,1024]{2,1,0:T(8,128)S(1)}, f32[2,128,1024]{2,1,0:T(8,128)S(1)}, u32[]{:S(2)}, u32[]{:S(2)}) %collective-permute-start.13) | collective-permute-done | bytes 1048608 | tf_op jit(solution)/shard_map/ppermute | solution.py:14
  167.9 4.5 %collective-permute-start.14 = (f32[2,128,1024]{2,1,0:T(8,128)}, f32[2,128,1024]{2,1,0:T(8,128)}, u32[]{:S(2)}, u32[]{:S(2)}) collective-permute-start(f32[2,128,1024]{2,1,0:T(8,128)} %maximum_add_fusion.5), channel_id=1, source_target_pairs={{0,1},{1,2},{2,3},{3,4},{4,5},{5,6},{6,7},{7,8},{8,9},{9,10},{10,1... | collective-permute-start | bytes 3145736 | tf_op jit(solution)/shard_map/ppermute | solution.py:14
  181.3 2.4 %maximum_add_fusion.3 = f32[2,128,1024]{2,1,0:T(8,128)} fusion(f32[2,128,1024]{2,1,0:T(8,128)} %collective-permute-done.10, f32[1,128,1024]{2,1,0:T(8,128)S(1)} %copy-done.75, f32[1,128,1024]{2,1,0:T(8,128)S(1)} %copy-done.73), kind=kLoop, calls=%fused_computation.106 | loop fusion | flops 524288 | bytes 3145728 | tf_op jit(solution)/shard_map/add | solution.py:119
  183.7 2.0 collective-permute-start.11
  185.7 9.9 %collective-permute-done.14 = f32[2,128,1024]{2,1,0:T(8,128)} collective-permute-done((f32[2,128,1024]{2,1,0:T(8,128)}, f32[2,128,1024]{2,1,0:T(8,128)}, u32[]{:S(2)}, u32[]{:S(2)}) %collective-permute-start.14) | collective-permute-done | bytes 1048608 | tf_op jit(solution)/shard_map/ppermute | solution.py:14
  195.7 2.4 %maximum_add_fusion.6 = f32[2,128,1024]{2,1,0:T(8,128)} fusion(f32[2,128,1024]{2,1,0:T(8,128)} %collective-permute-done.14, f32[1,128,1024]{2,1,0:T(8,128)S(1)} %copy-done.69, f32[1,128,1024]{2,1,0:T(8,128)S(1)} %copy-done.68), kind=kLoop, calls=%fused_computation.110 | loop fusion | flops 524288 | bytes 3145728 | tf_op jit(solution)/shard_map/add | solution.py:120
  198.0 4.5 %collective-permute-start.15 = (f32[2,128,1024]{2,1,0:T(8,128)}, f32[2,128,1024]{2,1,0:T(8,128)}, u32[]{:S(2)}, u32[]{:S(2)}) collective-permute-start(f32[2,128,1024]{2,1,0:T(8,128)} %maximum_add_fusion.6), channel_id=1, source_target_pairs={{0,1},{1,2},{2,3},{3,4},{4,5},{5,6},{6,7},{7,8},{8,9},{9,10},{10,1... | collective-permute-start | bytes 3145736 | tf_op jit(solution)/shard_map/ppermute | solution.py:14
  207.0 4.4 %collective-permute-done.11 = f32[2,128,1024]{2,1,0:T(8,128)} collective-permute-done((f32[2,128,1024]{2,1,0:T(8,128)}, f32[2,128,1024]{2,1,0:T(8,128)}, u32[]{:S(2)}, u32[]{:S(2)}) %collective-permute-start.11) | collective-permute-done | bytes 1048608 | tf_op jit(solution)/shard_map/ppermute | solution.py:14
  211.5 3.1 %collective-permute-done.15 = f32[2,128,1024]{2,1,0:T(8,128)} collective-permute-done((f32[2,128,1024]{2,1,0:T(8,128)}, f32[2,128,1024]{2,1,0:T(8,128)}, u32[]{:S(2)}, u32[]{:S(2)}) %collective-permute-start.15) | collective-permute-done | bytes 1048608 | tf_op jit(solution)/shard_map/ppermute | solution.py:14
  214.6 1.8 fusion.71
  (259 shorter events, 53.2 us)
Async XLA Ops:
  2.0 16.2 %copy-start.78 = (bf16[128,1024]{1,0:T(8,128)(2,1)S(1)}, bf16[128,1024]{1,0:T(8,128)(2,1)}, u32[]{:S(2)}) copy-start(bf16[128,1024]{1,0:T(8,128)(2,1)} %param.5) | copy-start | bytes 786436
  2.9 15.0 %copy-start.80 = (s32[2048]{0:T(1024)S(1)}, s32[2048]{0:T(1024)}, u32[]{:S(2)}) copy-start(s32[2048]{0:T(1024)} %param.9) | copy-start | bytes 24580
  2.9 16.8 %collective-permute-start = (bf16[2,128,1024]{1,2,0:T(8,128)(2,1)}, bf16[2,128,1024]{1,2,0:T(8,128)(2,1)}, u32[]{:S(2)}, u32[]{:S(2)}) collective-permute-start(bf16[2,128,1024]{1,2,0:T(8,128)(2,1)} %pad_maximum_fusion.2), channel_id=1, source_target_pairs={{0,4},{1,5},{2,6},{3,7},{4,8},{5,9},{6,10},{7,11},{8,12},{9,13},{1... | collective-permute-start | bytes 1572872 | tf_op jit(solution)/shard_map/ppermute | solution.py:14
  6.2 18.6 %collective-permute-start.6 = (bf16[2,128,1024]{1,2,0:T(8,128)(2,1)}, bf16[2,128,1024]{1,2,0:T(8,128)(2,1)S(1)}, u32[]{:S(2)}, u32[]{:S(2)}) collective-permute-start(bf16[2,128,1024]{1,2,0:T(8,128)(2,1)} %pad_maximum_fusion.2), channel_id=1, source_target_pairs={{3,0},{4,1},{5,2},{6,3},{7,4},{8,5},{9,6},{10,7},{11,8},{12,9},{13... | collective-permute-start | bytes 1572872 | tf_op jit(solution)/shard_map/ppermute | solution.py:14
  10.1 44.1 %collective-permute-start.5 = (bf16[2,128,1024]{1,2,0:T(8,128)(2,1)}, bf16[2,128,1024]{1,2,0:T(8,128)(2,1)}, u32[]{:S(2)}, u32[]{:S(2)}) collective-permute-start(bf16[2,128,1024]{1,2,0:T(8,128)(2,1)} %pad_maximum_fusion.2), channel_id=1, source_target_pairs={{2,0},{3,1},{4,2},{5,3},{6,4},{7,5},{8,6},{9,7},{10,8},{11,9},{12,... | collective-permute-start | bytes 1572872 | tf_op jit(solution)/shard_map/ppermute | solution.py:14
  12.2 45.0 %collective-permute-start.4 = (bf16[2,128,1024]{1,2,0:T(8,128)(2,1)}, bf16[2,128,1024]{1,2,0:T(8,128)(2,1)S(1)}, u32[]{:S(2)}, u32[]{:S(2)}) collective-permute-start(bf16[2,128,1024]{1,2,0:T(8,128)(2,1)} %pad_maximum_fusion.2), channel_id=1, source_target_pairs={{1,0},{2,1},{3,2},{4,3},{5,4},{6,5},{7,6},{8,7},{9,8},{10,9},{11,1... | collective-permute-start | bytes 1572872 | tf_op jit(solution)/shard_map/ppermute | solution.py:14
  14.7 42.9 %collective-permute-start.3 = (bf16[2,128,1024]{1,2,0:T(8,128)(2,1)}, bf16[2,128,1024]{1,2,0:T(8,128)(2,1)S(1)}, u32[]{:S(2)}, u32[]{:S(2)}) collective-permute-start(bf16[2,128,1024]{1,2,0:T(8,128)(2,1)} %pad_maximum_fusion.2), channel_id=1, source_target_pairs={{0,1},{1,2},{2,3},{3,4},{4,5},{5,6},{6,7},{7,8},{8,9},{9,10},{10,1... | collective-permute-start | bytes 1572872 | tf_op jit(solution)/shard_map/ppermute | solution.py:14
  19.4 5.4 %copy-start.27 = (bf16[16,8,8,128]{3,2,1,0:T(8,128)(2,1)}, bf16[16,8,8,128]{3,2,1,0:T(8,128)(2,1)S(1)}, u32[]{:S(2)}) copy-start(bf16[16,8,8,128]{3,2,1,0:T(8,128)(2,1)S(1)} %copy.324) | copy-start | bytes 786436
  19.7 39.3 %collective-permute-start.2 = (bf16[2,128,1024]{1,2,0:T(8,128)(2,1)}, bf16[2,128,1024]{1,2,0:T(8,128)(2,1)S(1)}, u32[]{:S(2)}, u32[]{:S(2)}) collective-permute-start(bf16[2,128,1024]{1,2,0:T(8,128)(2,1)} %pad_maximum_fusion.2), channel_id=1, source_target_pairs={{0,2},{1,3},{2,4},{3,5},{4,6},{5,7},{6,8},{7,9},{8,10},{9,11},{10,... | collective-permute-start | bytes 1572872 | tf_op jit(solution)/shard_map/ppermute | solution.py:14
  24.8 32.5 %copy-start.28 = (bf16[1,128,1024]{1,2,0:T(8,128)(2,1)}, bf16[1,128,1024]{1,2,0:T(8,128)(2,1)S(1)}, u32[]{:S(2)}) copy-start(bf16[1,128,1024]{1,2,0:T(8,128)(2,1)S(1)} %get-tuple-element.25) | copy-start | bytes 786436
  24.8 43.6 %copy-start.41 = (bf16[1,128,1024]{1,2,0:T(8,128)(2,1)}, bf16[1,128,1024]{1,2,0:T(8,128)(2,1)S(1)}, u32[]{:S(2)}) copy-start(bf16[1,128,1024]{1,2,0:T(8,128)(2,1)S(1)} %get-tuple-element.24) | copy-start | bytes 786436
  25.7 34.0 %collective-permute-start.1 = (bf16[2,128,1024]{1,2,0:T(8,128)(2,1)}, bf16[2,128,1024]{1,2,0:T(8,128)(2,1)S(1)}, u32[]{:S(2)}, u32[]{:S(2)}) collective-permute-start(bf16[2,128,1024]{1,2,0:T(8,128)(2,1)} %pad_maximum_fusion.2), channel_id=1, source_target_pairs={{0,3},{1,4},{2,5},{3,6},{4,7},{5,8},{6,9},{7,10},{8,11},{9,12},{10... | collective-permute-start | bytes 1572872 | tf_op jit(solution)/shard_map/ppermute | solution.py:14
  29.1 28.6 %copy-start.33 = (bf16[1,128,1024]{1,2,0:T(8,128)(2,1)}, bf16[1,128,1024]{1,2,0:T(8,128)(2,1)S(1)}, u32[]{:S(2)}) copy-start(bf16[1,128,1024]{1,2,0:T(8,128)(2,1)S(1)} %get-tuple-element.35) | copy-start | bytes 786436
  29.1 38.9 %copy-start.13 = (bf16[1,128,1024]{1,2,0:T(8,128)(2,1)}, bf16[1,128,1024]{1,2,0:T(8,128)(2,1)S(1)}, u32[]{:S(2)}) copy-start(bf16[1,128,1024]{1,2,0:T(8,128)(2,1)S(1)} %get-tuple-element.34) | copy-start | bytes 786436
  54.2 10.1 %collective-permute-start.7 = (bf16[2,128,1024]{1,2,0:T(8,128)(2,1)}, bf16[2,128,1024]{1,2,0:T(8,128)(2,1)S(1)}, u32[]{:S(2)}, u32[]{:S(2)}) collective-permute-start(bf16[2,128,1024]{1,2,0:T(8,128)(2,1)} %pad_maximum_fusion.2), channel_id=1, source_target_pairs={{4,0},{5,1},{6,2},{7,3},{8,4},{9,5},{10,6},{11,7},{12,8},{13,9},{1... | collective-permute-start | bytes 1572872 | tf_op jit(solution)/shard_map/ppermute | solution.py:14
  57.2 10.5 %copy-start.15 = (bf16[1,128,1024]{1,2,0:T(8,128)(2,1)}, bf16[1,128,1024]{1,2,0:T(8,128)(2,1)S(1)}, u32[]{:S(2)}) copy-start(bf16[1,128,1024]{1,2,0:T(8,128)(2,1)S(1)} %get-tuple-element.32) | copy-start | bytes 786436
  57.3 11.4 %copy-start.11 = (bf16[1,128,1024]{1,2,0:T(8,128)(2,1)}, bf16[1,128,1024]{1,2,0:T(8,128)(2,1)S(1)}, u32[]{:S(2)}) copy-start(bf16[1,128,1024]{1,2,0:T(8,128)(2,1)S(1)} %get-tuple-element.22) | copy-start | bytes 786436
  57.6 10.9 %copy-start.6 = (f32[8,128,128]{1,2,0:T(8,128)}, f32[8,128,128]{1,2,0:T(8,128)S(1)}, u32[]{:S(2)}) copy-start(f32[8,128,128]{1,2,0:T(8,128)S(1)} %get-tuple-element.74) | copy-start | bytes 1572868
  57.7 9.8 %copy-start.19 = (bf16[1,128,1024]{1,2,0:T(8,128)(2,1)}, bf16[1,128,1024]{1,2,0:T(8,128)(2,1)S(1)}, u32[]{:S(2)}) copy-start(bf16[1,128,1024]{1,2,0:T(8,128)(2,1)S(1)} %get-tuple-element.30) | copy-start | bytes 786436
  59.0 8.2 %copy-start.21 = (bf16[1,128,1024]{1,2,0:T(8,128)(2,1)}, bf16[1,128,1024]{1,2,0:T(8,128)(2,1)S(1)}, u32[]{:S(2)}) copy-start(bf16[1,128,1024]{1,2,0:T(8,128)(2,1)S(1)} %get-tuple-element.28) | copy-start | bytes 786436
  59.4 9.4 %copy-start.4 = (f32[8,128,128]{1,2,0:T(8,128)}, f32[8,128,128]{1,2,0:T(8,128)S(1)}, u32[]{:S(2)}) copy-start(f32[8,128,128]{1,2,0:T(8,128)S(1)} %get-tuple-element.64) | copy-start | bytes 1572868
  59.7 7.2 %copy-start.23 = (bf16[1,128,1024]{1,2,0:T(8,128)(2,1)}, bf16[1,128,1024]{1,2,0:T(8,128)(2,1)S(1)}, u32[]{:S(2)}) copy-start(bf16[1,128,1024]{1,2,0:T(8,128)(2,1)S(1)} %get-tuple-element.26) | copy-start | bytes 786436
  60.7 6.2 %copy-start = (f32[8,128,128]{1,2,0:T(8,128)}, f32[8,128,128]{1,2,0:T(8,128)S(1)}, u32[]{:S(2)}) copy-start(f32[8,128,128]{1,2,0:T(8,128)S(1)} %get-tuple-element.72) | copy-start | bytes 1572868
  64.4 3.8 %copy-start.25 = (bf16[1,128,1024]{1,2,0:T(8,128)(2,1)}, bf16[1,128,1024]{1,2,0:T(8,128)(2,1)S(1)}, u32[]{:S(2)}) copy-start(bf16[1,128,1024]{1,2,0:T(8,128)(2,1)S(1)} %get-tuple-element.37) | copy-start | bytes 786436
  65.1 3.1 %copy-start.2 = (f32[8,128,128]{1,2,0:T(8,128)}, f32[8,128,128]{1,2,0:T(8,128)S(1)}, u32[]{:S(2)}) copy-start(f32[8,128,128]{1,2,0:T(8,128)S(1)} %get-tuple-element.58) | copy-start | bytes 1572868
  76.7 12.6 %copy-start.17 = (bf16[8,128,128]{1,2,0:T(8,128)(2,1)}, bf16[8,128,128]{1,2,0:T(8,128)(2,1)S(1)}, u32[]{:S(2)}) copy-start(bf16[8,128,128]{1,2,0:T(8,128)(2,1)S(1)} %fusion.59) | copy-start | bytes 786436
  83.9 26.3 %copy-start.31 = (bf16[8,128,128]{1,2,0:T(8,128)(2,1)}, bf16[8,128,128]{1,2,0:T(8,128)(2,1)S(1)}, u32[]{:S(2)}) copy-start(bf16[8,128,128]{1,2,0:T(8,128)(2,1)S(1)} %fusion.64) | copy-start | bytes 786436
  93.5 4.5 %copy-start.30 = (bf16[8,128,128]{1,2,0:T(8,128)(2,1)S(1)}, bf16[8,128,128]{1,2,0:T(8,128)(2,1)}, u32[]{:S(2)}) copy-start(bf16[8,128,128]{1,2,0:T(8,128)(2,1)} %fusion.62) | copy-start | bytes 786436
  95.9 31.5 %collective-permute-start.8 = (f32[2,128,1024]{2,1,0:T(8,128)}, f32[2,128,1024]{2,1,0:T(8,128)}, u32[]{:S(2)}, u32[]{:S(2)}) collective-permute-start(f32[2,128,1024]{2,1,0:T(8,128)} %pad_maximum_fusion), channel_id=1, source_target_pairs={{1,0},{2,1},{3,2},{4,3},{5,4},{6,5},{7,6},{8,7},{9,8},{10,9},{11,1... | collective-permute-start | bytes 3145736 | tf_op jit(solution)/shard_map/ppermute | solution.py:14
  105.6 25.2 %collective-permute-start.12 = (f32[2,128,1024]{2,1,0:T(8,128)}, f32[2,128,1024]{2,1,0:T(8,128)}, u32[]{:S(2)}, u32[]{:S(2)}) collective-permute-start(f32[2,128,1024]{2,1,0:T(8,128)} %pad_maximum_fusion.1), channel_id=1, source_target_pairs={{0,1},{1,2},{2,3},{3,4},{4,5},{5,6},{6,7},{7,8},{8,9},{9,10},{10,1... | collective-permute-start | bytes 3145736 | tf_op jit(solution)/shard_map/ppermute | solution.py:14
  127.4 3.5 %copy-start.70 = (f32[1,128,1024]{2,1,0:T(8,128)S(1)}, f32[1,128,1024]{2,1,0:T(8,128)}, u32[]{:S(2)}) copy-start(f32[1,128,1024]{2,1,0:T(8,128)} %copy.245) | copy-start | bytes 1572868
  127.4 3.5 %copy-start.71 = (f32[1,128,1024]{2,1,0:T(8,128)S(1)}, f32[1,128,1024]{2,1,0:T(8,128)}, u32[]{:S(2)}) copy-start(f32[1,128,1024]{2,1,0:T(8,128)} %copy.246) | copy-start | bytes 1572868
  128.9 27.4 %collective-permute-start.9 = (f32[2,128,1024]{2,1,0:T(8,128)S(1)}, f32[2,128,1024]{2,1,0:T(8,128)S(1)}, u32[]{:S(2)}, u32[]{:S(2)}) collective-permute-start(f32[2,128,1024]{2,1,0:T(8,128)S(1)} %maximum_add_fusion.1), channel_id=1, source_target_pairs={{1,0},{2,1},{3,2},{4,3},{5,4},{6,5},{7,6},{8,7},{9,8},{10,9},{11,1... | collective-permute-start | bytes 3145736 | tf_op jit(solution)/shard_map/ppermute | solution.py:14
  132.2 34.5 %collective-permute-start.13 = (f32[2,128,1024]{2,1,0:T(8,128)S(1)}, f32[2,128,1024]{2,1,0:T(8,128)S(1)}, u32[]{:S(2)}, u32[]{:S(2)}) collective-permute-start(f32[2,128,1024]{2,1,0:T(8,128)S(1)} %maximum_add_fusion.4), channel_id=1, source_target_pairs={{0,1},{1,2},{2,3},{3,4},{4,5},{5,6},{6,7},{7,8},{8,9},{9,10},{10,1... | collective-permute-start | bytes 3145736 | tf_op jit(solution)/shard_map/ppermute | solution.py:14
  138.1 18.2 %copy-start.66 = (f32[1,128,1024]{2,1,0:T(8,128)S(1)}, f32[1,128,1024]{2,1,0:T(8,128)}, u32[]{:S(2)}) copy-start(f32[1,128,1024]{2,1,0:T(8,128)} %copy.227) | copy-start | bytes 1572868
  138.1 18.2 %copy-start.67 = (f32[1,128,1024]{2,1,0:T(8,128)S(1)}, f32[1,128,1024]{2,1,0:T(8,128)}, u32[]{:S(2)}) copy-start(f32[1,128,1024]{2,1,0:T(8,128)} %copy.228) | copy-start | bytes 1572868
  138.3 28.4 %copy-start.64 = (f32[1,128,1024]{2,1,0:T(8,128)S(1)}, f32[1,128,1024]{2,1,0:T(8,128)}, u32[]{:S(2)}) copy-start(f32[1,128,1024]{2,1,0:T(8,128)} %copy.251) | copy-start | bytes 1572868
  138.3 28.4 %copy-start.65 = (f32[1,128,1024]{2,1,0:T(8,128)S(1)}, f32[1,128,1024]{2,1,0:T(8,128)}, u32[]{:S(2)}) copy-start(f32[1,128,1024]{2,1,0:T(8,128)} %copy.252) | copy-start | bytes 1572868
  157.4 23.0 %collective-permute-start.10 = (f32[2,128,1024]{2,1,0:T(8,128)}, f32[2,128,1024]{2,1,0:T(8,128)}, u32[]{:S(2)}, u32[]{:S(2)}) collective-permute-start(f32[2,128,1024]{2,1,0:T(8,128)} %maximum_add_fusion.2), channel_id=1, source_target_pairs={{1,0},{2,1},{3,2},{4,3},{5,4},{6,5},{7,6},{8,7},{9,8},{10,9},{11,1... | collective-permute-start | bytes 3145736 | tf_op jit(solution)/shard_map/ppermute | solution.py:14
  167.9 4.8 %copy-start.52 = (f32[8,128,128]{1,2,0:T(8,128)S(1)}, f32[8,128,128]{1,2,0:T(8,128)}, u32[]{:S(2)}) copy-start(f32[8,128,128]{1,2,0:T(8,128)} %fusion.145) | copy-start | bytes 1572868
  167.9 27.8 %collective-permute-start.14 = (f32[2,128,1024]{2,1,0:T(8,128)}, f32[2,128,1024]{2,1,0:T(8,128)}, u32[]{:S(2)}, u32[]{:S(2)}) collective-permute-start(f32[2,128,1024]{2,1,0:T(8,128)} %maximum_add_fusion.5), channel_id=1, source_target_pairs={{0,1},{1,2},{2,3},{3,4},{4,5},{5,6},{6,7},{7,8},{8,9},{9,10},{10,1... | collective-permute-start | bytes 3145736 | tf_op jit(solution)/shard_map/ppermute | solution.py:14
  180.3 15.3 %copy-start.68 = (f32[1,128,1024]{2,1,0:T(8,128)S(1)}, f32[1,128,1024]{2,1,0:T(8,128)}, u32[]{:S(2)}) copy-start(f32[1,128,1024]{2,1,0:T(8,128)} %copy.257) | copy-start | bytes 1572868
  180.4 15.3 %copy-start.69 = (f32[1,128,1024]{2,1,0:T(8,128)S(1)}, f32[1,128,1024]{2,1,0:T(8,128)}, u32[]{:S(2)}) copy-start(f32[1,128,1024]{2,1,0:T(8,128)} %copy.258) | copy-start | bytes 1572868
  183.7 18.9 %copy-start.34 = (bf16[1,128,1024]{1,2,0:T(8,128)(2,1)S(1)}, bf16[1,128,1024]{1,2,0:T(8,128)(2,1)}, u32[]{:S(2)}) copy-start(bf16[1,128,1024]{1,2,0:T(8,128)(2,1)} %copy-done.33) | copy-start | bytes 786436
  183.7 27.8 %collective-permute-start.11 = (f32[2,128,1024]{2,1,0:T(8,128)}, f32[2,128,1024]{2,1,0:T(8,128)}, u32[]{:S(2)}, u32[]{:S(2)}) collective-permute-start(f32[2,128,1024]{2,1,0:T(8,128)} %maximum_add_fusion.3), channel_id=1, source_target_pairs={{1,0},{2,1},{3,2},{4,3},{5,4},{6,5},{7,6},{8,7},{9,8},{10,9},{11,1... | collective-permute-start | bytes 3145736 | tf_op jit(solution)/shard_map/ppermute | solution.py:14
  198.0 4.8 %copy-start.40 = (bf16[1,128,1024]{1,2,0:T(8,128)(2,1)S(1)}, bf16[1,128,1024]{1,2,0:T(8,128)(2,1)}, u32[]{:S(2)}) copy-start(bf16[1,128,1024]{1,2,0:T(8,128)(2,1)} %copy-done.39) | copy-start | bytes 786436
  198.0 16.6 %collective-permute-start.15 = (f32[2,128,1024]{2,1,0:T(8,128)}, f32[2,128,1024]{2,1,0:T(8,128)}, u32[]{:S(2)}, u32[]{:S(2)}) collective-permute-start(f32[2,128,1024]{2,1,0:T(8,128)} %maximum_add_fusion.6), channel_id=1, source_target_pairs={{0,1},{1,2},{2,3},{3,4},{4,5},{5,6},{6,7},{7,8},{8,9},{9,10},{10,1... | collective-permute-start | bytes 3145736 | tf_op jit(solution)/shard_map/ppermute | solution.py:14
  205.3 9.3 %copy-start.51 = (f32[1,128,1024]{2,1,0:T(8,128)S(1)}, f32[1,128,1024]{2,1,0:T(8,128)}, u32[]{:S(2)}) copy-start(f32[1,128,1024]{2,1,0:T(8,128)} %copy.210) | copy-start | bytes 1572868
  (49 other events, 62.1 us)
where the time goes:
time: 220 us; the launch traced here: 217 us
  waiting for transfers between devices  72.3 us (33%)
  starting transfers between devices  47.2 us (21%)
  local copies, waits for them, and re-layouts  43.5 us (20%)
  matrix products  32.9 us (15%)
  other arithmetic  19.4 us (9%)
    ppermute x16, waiting for transfers between devices, passed_along(): lax.ppermute(value, axis, [(source, source + steps) for source in range(l...  72.3 us
    ppermute x16, starting transfers between devices, passed_along(): lax.ppermute(value, axis, [(source, source + steps) for source in range(l...  47.2 us
    another operation x18, local copies, waits for them, and re-layouts, shards(): jnp.stack((key_part.reshape(row_count, features), value_part.reshape(row_...  25.1 us
    unnamed x168, local copies, waits for them, and re-layouts  13.7 us
    dot_general x9, matrix products, shards(): jnp.einsum('hqk,qhd->khd', weights.astype(jnp.bfloat16), grad_heads, pref...  11.2 us
    dot_general x9, matrix products, shards(): jnp.einsum('hqk,qhd->khd', grad_scores, query_heads, preferred_element_ty...  9.09 us
    add x3, other arithmetic, shards(): carried_down + parts[REACH - distance]  4.89 us
    add x3, other arithmetic, shards(): carried_up = passed_along(carried_up + parts[REACH + distance], 'seq', 1)  4.84 us
  transfers between devices with their start and end apart: 16, of which 8 were waited for; matrix products, arithmetic and copies ran while one was open for 25% of the time, Pallas kernels for 0%

commit v1 on v0

v1 whole, which is shorter than its diff:
```python
import functools

import jax
import jax.numpy as jnp
from jax import lax
from jax.experimental import pallas as pl
from jax.experimental.pallas import tpu as pltpu
from jax.sharding import PartitionSpec as P

HEAD = 128
REACH = 4
ROWS = 128
PAIR = 2
TILE = 256
SCALING = HEAD ** (-0.5)
AWAY = -1e30
NOBODY = 127
BF = jnp.bfloat16
F32 = jnp.float32


def dot(left, right):
    return jnp.dot(left, right, preferred_element_type=F32)


def kernel(
    slabs,
    q_in, k_in, v_in, g_in, session,
    att_out, dq_out, dk_out, dv_out,
    kx, vw, qs, gs, qtx, gt, vt, kt, scores, acc,
    stage, arrived, small, final,
    own_sem, in_send, in_recv, z_send, z_recv, gz_send, gz_recv, out_own, out_send, out_recv,
):
    me = lax.axis_index("seq")
    slab, place = me // REACH, me % REACH
    side, core = place // 2, place % 2
    has_low, has_high = slab > 0, slab < slabs - 1

    def partner(d):
        return 2 * ((side + d // 2) % 2) + (core + d % 2) % 2

    def columns(of, h):
        return pl.ds(pl.multiple_of((PAIR * of + h) * HEAD, HEAD), HEAD)

    def remote(src, dst, send, recv, device):
        return pltpu.make_async_remote_copy(
            src_ref=src, dst_ref=dst, send_sem=send, recv_sem=recv,
            device_id={"seq": device}, device_id_type=pl.DeviceIdType.MESH,
        )

    def landing(t, h, block):
        if t == 0:
            return kx.at[h, block, :, pl.ds(0, HEAD)]
        return vw.at[h, block]

    def slab_landing(t, h, block):
        if t < 2:
            return landing(t, h, REACH + block)
        return (qs if t == 2 else gs).at[h, block]

    sources = (k_in, v_in, q_in, g_in)
    results = (att_out, dq_out, dk_out, dv_out)

    def in_copy(t, h, d, sending):
        other = partner(d)
        if sending:
            return remote(sources[t].at[:, columns(other, h)], slab_landing(t, h, place),
                          in_send.at[t, h, d - 1], in_recv.at[t, h, d - 1], slab * REACH + other)
        return remote(slab_landing(t, h, other), slab_landing(t, h, other),
                      in_send.at[t, h, d - 1], in_recv.at[t, h, d - 1], slab * REACH + other)

    def own_copy(t, h):
        return pltpu.make_async_copy(
            sources[t].at[:, columns(place, h)], slab_landing(t, h, place), own_sem.at[t, h])

    def z_copy(way, t, h, d):
        block = partner(d)
        src = sources[t].at[:, columns(place, h)] if d == 0 else landing(t, h, REACH + block)
        dst = landing(t, h, block + (2 * REACH if way == 0 else 0))
        return remote(src, dst, z_send.at[way, t, h, d], z_recv.at[way, t, h, d],
                      me + (-REACH if way == 0 else REACH))

    def gz_copy(way, h, part):
        return remote(stage.at[way, h, part], arrived.at[way, h, part],
                      gz_send.at[way, h, part], gz_recv.at[way, h, part],
                      me + (-REACH if way == 0 else REACH))

    def out_source(t, h, block):
        return small.at[t, h, block] if t < 2 else final.at[t - 2, h, block]

    def out_copy(t, h, d):
        other = partner(d)
        return remote(out_source(t, h, other), results[t].at[:, columns(place, h)],
                      out_send.at[t, h, d - 1], out_recv.at[t, h, d - 1], slab * REACH + other)

    def out_arrival(t, h, d):
        other = partner(d)
        dst = results[t].at[:, columns(other, h)]
        return remote(out_source(t, h, other), dst,
                      out_send.at[t, h, d - 1], out_recv.at[t, h, d - 1], slab * REACH + other)

    def out_own_copy(t, h):
        return pltpu.make_async_copy(
            out_source(t, h, place), results[t].at[:, columns(place, h)], out_own.at[t, h])

    def both_ways(action):
        @pl.when(has_low)
        def _():
            action(0)

        @pl.when(has_high)
        def _():
            action(1)

    barrier = pltpu.get_barrier_semaphore()
    for d in (1, 2, 3):
        pl.semaphore_signal(barrier, inc=1, device_id={"seq": slab * REACH + partner(d)},
                            device_id_type=pl.DeviceIdType.MESH)

    def greet(way):
        pl.semaphore_signal(barrier, inc=1, device_id={"seq": me + (-REACH if way == 0 else REACH)},
                            device_id_type=pl.DeviceIdType.MESH)

    both_ways(greet)
    for h in range(PAIR):
        for t in (0, 1, 2, 3):
            own_copy(t, h).start()
    pl.semaphore_wait(barrier, 3 + has_low.astype(jnp.int32) + has_high.astype(jnp.int32))

    for h in range(PAIR):
        for d in (2, 3, 1):
            for t in (0, 1):
                in_copy(t, h, d, True).start()
        for t in (0, 1):
            both_ways(lambda way: z_copy(way, t, h, 0).start())
        for d in (2, 3, 1):
            for t in (2, 3):
                in_copy(t, h, d, True).start()

    rows = lax.broadcasted_iota(jnp.int32, (ROWS, ROWS), 0)
    for w in range(3 * REACH):
        block = slab * REACH - REACH + w
        inside = jnp.logical_and(block >= 0, block < slabs * REACH)
        held = session[pl.ds(jnp.clip(block, 0, slabs * REACH - 1), 1), :]
        held = jnp.where(inside, held, NOBODY)
        hot = jnp.where(rows == held, 1.0, 0.0).astype(F32).T.astype(BF)
        for h in range(PAIR):
            kx[h, w, :, HEAD:] = hot
    for block in range(REACH):
        held = session[pl.ds(slab * REACH + block, 1), :]
        away = jnp.where(rows == held, 0.0, AWAY).astype(BF)
        at = (block % 2) * ROWS
        for h in range(PAIR):
            qtx[h, block // 2, HEAD:, at:at + ROWS] = away
    acc[...] = jnp.zeros_like(acc)

    def empty(way):
        first = 0 if way == 0 else 2 * REACH
        zeros = jnp.zeros((PAIR, REACH, ROWS, HEAD), BF)
        kx[:, first:first + REACH, :, :HEAD] = zeros
        vw[:, first:first + REACH] = zeros
        arrived[1 - way] = jnp.zeros(arrived.shape[1:], BF)

    pl.when(jnp.logical_not(has_low))(lambda: empty(0))
    pl.when(jnp.logical_not(has_high))(lambda: empty(1))

    for h in range(PAIR):
        for d in (1, 2, 3):
            for t in (0, 1):
                in_copy(t, h, d, False).wait_recv()
                both_ways(lambda way: z_copy(way, t, h, d).start())

    def chunk(h, c):
        q = qs[h, 2 * c:2 * c + 2].reshape(TILE, HEAD)
        g = gs[h, 2 * c:2 * c + 2].reshape(TILE, HEAD)
        g_t = gt[c]
        high = None
        for i in range(5):
            w = 2 * (c + i)
            s = dot(kx[h, w:w + 2].reshape(TILE, 2 * HEAD), qtx[h, c])
            scores[i] = s
            top = jnp.max(s, axis=0, keepdims=True)
            high = top if high is None else jnp.maximum(high, top)
        total = jnp.zeros((1, TILE), F32)
        for i in range(5):
            e = jnp.exp((scores[i] - high) * SCALING)
            scores[i] = e
            total = total + jnp.sum(e, axis=0, keepdims=True)
        share = 1.0 / total
        att = jnp.zeros((HEAD, TILE), F32)
        for i in range(5):
            p = scores[i] * share
            scores[i] = p
            p = p.astype(BF)
            att = att + dot(vt[c + i], p)
            acc[h, c + i, 1] += dot(p, g)
        att = att.astype(BF).astype(F32)
        delta = jnp.sum(g_t.astype(F32) * att, axis=0, keepdims=True)
        small[0, h, 2 * c:2 * c + 2] = att.T.astype(BF).reshape(2, ROWS, HEAD)
        dq = jnp.zeros((HEAD, TILE), F32)
        for i in range(5):
            w = 2 * (c + i)
            dp = dot(vw[h, w:w + 2].reshape(TILE, HEAD), g_t)
            ds = (scores[i] * (dp - delta) * SCALING).astype(BF)
            dq = dq + dot(kt[c + i], ds)
            acc[h, c + i, 0] += dot(ds, q)
        small[1, h, 2 * c:2 * c + 2] = dq.T.astype(BF).reshape(2, ROWS, HEAD)

    def finish(h):
        for part in range(2):
            pl.when(has_high)(lambda: gz_copy(0, h, part).wait_recv())
            pl.when(has_low)(lambda: gz_copy(1, h, part).wait_recv())
            for t in range(2):
                whole = (acc[h, 2 + part, t] + arrived[0, h, part, t].astype(F32)
                         + arrived[1, h, part, t].astype(F32))
                final[t, h, 2 * part:2 * part + 2] = whole.astype(BF).reshape(2, ROWS, HEAD)
        for t in (2, 3):
            for d in (2, 3, 1):
                out_copy(t, h, d).start()
            out_own_copy(t, h).start()

    def head(h, carry):
        for t in range(4):
            own_copy(t, h).wait()
            if t >= 2:
                for d in (1, 2, 3):
                    in_copy(t, h, d, False).wait_recv()
        for c in range(2):
            at = slice(2 * c, 2 * c + 2)
            qtx[h, c, :HEAD] = qs[h, at].reshape(TILE, HEAD).T
            gt[c] = gs[h, at].reshape(TILE, HEAD).T

        def window_arrival(way):
            for t in range(2):
                for d in range(4):
                    block = partner(d) + (0 if way == 0 else 2 * REACH)
                    remote(landing(t, h, block), landing(t, h, block), z_send.at[1 - way, t, h, d],
                           z_recv.at[1 - way, t, h, d], me + (-REACH if way == 0 else REACH)).wait_recv()

        both_ways(window_arrival)
        for i in range(6):
            vt[i] = vw[h, 2 * i:2 * i + 2].reshape(TILE, HEAD).T
            kt[i] = kx[h, 2 * i:2 * i + 2, :, :HEAD].reshape(TILE, HEAD).T
        chunk(h, 0)
        stage[0, h, 0] = acc[h, 0].astype(BF)
        pl.when(has_low)(lambda: gz_copy(0, h, 0).start())
        pl.when(h == 1)(lambda: finish(0))
        chunk(h, 1)
        stage[0, h, 1] = acc[h, 1].astype(BF)
        pl.when(has_low)(lambda: gz_copy(0, h, 1).start())
        for part in range(2):
            stage[1, h, part] = acc[h, 4 + part].astype(BF)
            pl.when(has_high)(lambda: gz_copy(1, h, part).start())
        for t in range(2):
            for d in (2, 3, 1):
                out_copy(t, h, d).start()
            out_own_copy(t, h).start()
        return carry

    lax.fori_loop(0, PAIR, head, 0)
    finish(1)

    for h in range(PAIR):
        for t in range(4):
            for d in (1, 2, 3):
                in_copy(t, h, d, True).wait_send()
                out_copy(t, h, d).wait_send()
                out_arrival(t, h, d).wait_recv()
            out_own_copy(t, h).wait()

        def sent(way):
            for t in range(2):
                for d in range(4):
                    z_copy(way, t, h, d).wait_send()
            for part in range(2):
                gz_copy(way, h, part).wait_send()

        both_ways(sent)


def shards(slabs, query, key, value, out_grad, session):
    rows, features = query.shape
    dma = pltpu.SemaphoreType.DMA
    result = jax.ShapeDtypeStruct((rows, features), BF)
    return pl.pallas_call(
        functools.partial(kernel, slabs),
        out_shape=(result,) * 4,
        in_specs=[pl.BlockSpec(memory_space=pl.ANY)] * 4 + [pl.BlockSpec(memory_space=pltpu.VMEM)],
        out_specs=(pl.BlockSpec(memory_space=pl.ANY),) * 4,
        scratch_shapes=[
            pltpu.VMEM((PAIR, 3 * REACH, ROWS, 2 * HEAD), BF),
            pltpu.VMEM((PAIR, 3 * REACH, ROWS, HEAD), BF),
            pltpu.VMEM((PAIR, REACH, ROWS, HEAD), BF),
            pltpu.VMEM((PAIR, REACH, ROWS, HEAD), BF),
            pltpu.VMEM((PAIR, 2, 2 * HEAD, TILE), BF),
            pltpu.VMEM((2, HEAD, TILE), BF),
            pltpu.VMEM((6, HEAD, TILE), BF),
            pltpu.VMEM((6, HEAD, TILE), BF),
            pltpu.VMEM((5, TILE, TILE), F32),
            pltpu.VMEM((PAIR, 6, 2, TILE, HEAD), F32),
            pltpu.VMEM((2, PAIR, 2, 2, TILE, HEAD), BF),
            pltpu.VMEM((2, PAIR, 2, 2, TILE, HEAD), BF),
            pltpu.VMEM((2, PAIR, REACH, ROWS, HEAD), BF),
            pltpu.VMEM((2, PAIR, REACH, ROWS, HEAD), BF),
            dma((4, PAIR)),
            dma((4, PAIR, 3)),
            dma((4, PAIR, 3)),
            dma((2, 2, PAIR, 4)),
            dma((2, 2, PAIR, 4)),
            dma((2, PAIR, 2)),
            dma((2, PAIR, 2)),
            dma((4, PAIR)),
            dma((4, PAIR, 3)),
            dma((4, PAIR, 3)),
        ],
        compiler_params=pltpu.CompilerParams(
            collective_id=0, has_side_effects=True, vmem_limit_bytes=40 * 1024 * 1024),
        cost_estimate=pl.CostEstimate(
            flops=2_000_000_000, bytes_accessed=2_100_000, transcendentals=1_300_000),
    )(query, key, value, out_grad, session.reshape(-1, ROWS))


def solution(mesh):
    split = P(("groups", "seq"), None)
    return jax.shard_map(
        functools.partial(shards, mesh.shape["seq"] // REACH),
        mesh=mesh,
        in_specs=(split, split, split, split, P("groups")),
        out_specs=(split,) * 4,
        check_vma=False,
    )
```

time: 220 us -> 47.5 us (0.22); the launches traced: 217 us -> 47.2 us
  waiting for transfers between devices: 72.3 us -> 0 us
  starting transfers between devices: 47.2 us -> 0 us
  Pallas kernels: 0 us -> 39.3 us
  local copies, waits for them, and re-layouts: 43.5 us -> 7.3 us
  matrix products: 32.9 us -> 0 us
  other arithmetic: 19.4 us -> 0 us
    ppermute x16 -> x0, waiting for transfers between devices: 72.3 us -> none  [passed_along(): lax.ppermute(value, axis, [(source, source + steps) for source in range(l...]
    ppermute x16 -> x0, starting transfers between devices: 47.2 us -> none  [passed_along(): lax.ppermute(value, axis, [(source, source + steps) for source in range(l...]
    pallas_call x0 -> x1, Pallas kernels: none -> 39.3 us  [shards(): pl.pallas_call(functools.partial(kernel, slabs), out_shape=(result,) * 4,...]
    dot_general x54 -> x0, matrix products: 32.9 us -> none  [the longest x9 11.2 us: shards(): jnp.einsum('hqk,qhd->khd', weights.astype(jnp.bfloat16), grad_heads, pref...]
    another operation x18 -> x0, local copies, waits for them, and re-layouts: 25.1 us -> none  [shards(): jnp.stack((key_part.reshape(row_count, features), value_part.reshape(row_...]
    add x7 -> x0, other arithmetic: 9.77 us -> none  [the longest x3 4.89 us: shards(): carried_down + parts[REACH - distance]]
    another operation x4 -> x0, other arithmetic: 7.27 us -> none  [the longest x2 4.66 us: shards(): jnp.stack((key_part.reshape(row_count, features), value_part.reshape(row_...]
    unnamed x168 -> x14, local copies, waits for them, and re-layouts: 13.7 us -> 7.3 us
  transfers between devices with their start and end apart: 16 -> 0, of which waited for: 8 -> 0; matrix products, arithmetic and copies ran while one was open for 25% -> 0% of each run, Pallas kernels for 0% -> 0%
where the time goes in v1:
time: 47.5 us; the launch traced here: 47.2 us
  Pallas kernels  39.3 us (83%)
  local copies, waits for them, and re-layouts  7.3 us (15%)
  between operations  0.65 us (1%)
    pallas_call x1, Pallas kernels, shards(): pl.pallas_call(functools.partial(kernel, slabs), out_shape=(result,) * 4,...  39.3 us
    unnamed x14, local copies, waits for them, and re-layouts  7.3 us

profile of v1, /device:TPU:17, one launch (start us, length us, event | category | flops | bytes accessed | tf_op | source)
XLA Modules:
  0.0 47.2 jit_solution(782686403957242154)
XLA Ops:
  0.6 0.0 copy-start
  0.6 0.9 %copy-done = bf16[128,1024]{1,0:T(8,128)(2,1)S(1)} copy-done((bf16[128,1024]{1,0:T(8,128)(2,1)S(1)}, bf16[128,1024]{1,0:T(8,128)(2,1)}, u32[]{:S(2)}) %copy-start) | copy-done | bytes 262168
  1.6 0.0 copy-start.1
  1.6 0.9 %copy-done.1 = bf16[128,1024]{1,0:T(8,128)(2,1)S(1)} copy-done((bf16[128,1024]{1,0:T(8,128)(2,1)S(1)}, bf16[128,1024]{1,0:T(8,128)(2,1)}, u32[]{:S(2)}) %copy-start.1) | copy-done | bytes 262168
  2.5 0.0 copy-start.2
  2.5 0.9 %copy-done.2 = bf16[128,1024]{1,0:T(8,128)(2,1)S(1)} copy-done((bf16[128,1024]{1,0:T(8,128)(2,1)S(1)}, bf16[128,1024]{1,0:T(8,128)(2,1)}, u32[]{:S(2)}) %copy-start.2) | copy-done | bytes 262168
  3.5 0.0 copy-start.3
  3.5 0.9 %copy-done.3 = bf16[128,1024]{1,0:T(8,128)(2,1)S(1)} copy-done((bf16[128,1024]{1,0:T(8,128)(2,1)S(1)}, bf16[128,1024]{1,0:T(8,128)(2,1)}, u32[]{:S(2)}) %copy-start.3) | copy-done | bytes 262168
  4.4 0.0 copy-start.4
  4.4 0.7 %copy-done.4 = s32[2048]{0:T(1024)S(1)} copy-done((s32[2048]{0:T(1024)S(1)}, s32[2048]{0:T(1024)}, u32[]{:S(2)}) %copy-start.4) | copy-done | bytes 8216
  5.1 39.3 %shard_map.84 = (bf16[128,1024]{1,0:T(8,128)(2,1)S(1)}, bf16[128,1024]{1,0:T(8,128)(2,1)S(1)}, bf16[128,1024]{1,0:T(8,128)(2,1)S(1)}, bf16[128,1024]{1,0:T(8,128)(2,1)S(1)}) custom-call(bf16[128,1024]{1,0:T(8,128)(2,1)S(1)} %copy-done, bf16[128,1024]{1,0:T(8,128)(2,1)S(1)} %copy-done.1, bf16[128,1024]{1,0:T(8,128)(2,1)S(1)} %copy-done.2, ...), custom_call_target="tpu_custom_call" | custom-call | flops 2000000000 | bytes 2100000 | tf_op jit(solution)/shard_map/pallas_call | solution.py:285
  44.4 0.7 %copy.13 = bf16[128,1024]{1,0:T(8,128)(2,1)} copy(bf16[128,1024]{1,0:T(8,128)(2,1)S(1)} %get-tuple-element.8) | data formatting | bytes 524288
  45.1 0.7 %copy.14 = bf16[128,1024]{1,0:T(8,128)(2,1)} copy(bf16[128,1024]{1,0:T(8,128)(2,1)S(1)} %get-tuple-element.9) | data formatting | bytes 524288
  45.8 0.7 %copy.15 = bf16[128,1024]{1,0:T(8,128)(2,1)} copy(bf16[128,1024]{1,0:T(8,128)(2,1)S(1)} %get-tuple-element.10) | data formatting | bytes 524288
  46.5 0.7 %copy.16 = bf16[128,1024]{1,0:T(8,128)(2,1)} copy(bf16[128,1024]{1,0:T(8,128)(2,1)S(1)} %get-tuple-element.11) | data formatting | bytes 524288
Async XLA Ops:
  0.6 1.0 %copy-start = (bf16[128,1024]{1,0:T(8,128)(2,1)S(1)}, bf16[128,1024]{1,0:T(8,128)(2,1)}, u32[]{:S(2)}) copy-start(bf16[128,1024]{1,0:T(8,128)(2,1)} %q_in.1) | copy-start | bytes 786436
  1.6 0.9 %copy-start.1 = (bf16[128,1024]{1,0:T(8,128)(2,1)S(1)}, bf16[128,1024]{1,0:T(8,128)(2,1)}, u32[]{:S(2)}) copy-start(bf16[128,1024]{1,0:T(8,128)(2,1)} %k_in.1) | copy-start | bytes 786436
  2.5 0.9 %copy-start.2 = (bf16[128,1024]{1,0:T(8,128)(2,1)S(1)}, bf16[128,1024]{1,0:T(8,128)(2,1)}, u32[]{:S(2)}) copy-start(bf16[128,1024]{1,0:T(8,128)(2,1)} %v_in.1) | copy-start | bytes 786436
  3.5 0.9 %copy-start.3 = (bf16[128,1024]{1,0:T(8,128)(2,1)S(1)}, bf16[128,1024]{1,0:T(8,128)(2,1)}, u32[]{:S(2)}) copy-start(bf16[128,1024]{1,0:T(8,128)(2,1)} %g_in.1) | copy-start | bytes 786436
  4.4 0.7 %copy-start.4 = (s32[2048]{0:T(1024)S(1)}, s32[2048]{0:T(1024)}, u32[]{:S(2)}) copy-start(s32[2048]{0:T(1024)} %param.9) | copy-start | bytes 24580

commit v2 on v1

--- a/solution.py
+++ b/solution.py
@@ -127,15 +127,23 @@
             own_copy(t, h).start()
     pl.semaphore_wait(barrier, 3 + has_low.astype(jnp.int32) + has_high.astype(jnp.int32))
 
-    for h in range(PAIR):
-        for d in (2, 3, 1):
+    def send_inputs(h):
+        for d in (2, 3):
             for t in (0, 1):
                 in_copy(t, h, d, True).start()
         for t in (0, 1):
+            in_copy(t, h, 1, True).start()
             both_ways(lambda way: z_copy(way, t, h, 0).start())
         for d in (2, 3, 1):
             for t in (2, 3):
                 in_copy(t, h, d, True).start()
+
+    def relay(h, d):
+        for t in (0, 1):
+            in_copy(t, h, d, False).wait_recv()
+            both_ways(lambda way: z_copy(way, t, h, d).start())
+
+    send_inputs(0)
 
     rows = lax.broadcasted_iota(jnp.int32, (ROWS, ROWS), 0)
     for w in range(3 * REACH):
@@ -152,8 +160,6 @@
         at = (block % 2) * ROWS
         for h in range(PAIR):
             qtx[h, block // 2, HEAD:, at:at + ROWS] = away
-    acc[...] = jnp.zeros_like(acc)
-
     def empty(way):
         first = 0 if way == 0 else 2 * REACH
         zeros = jnp.zeros((PAIR, REACH, ROWS, HEAD), BF)
@@ -164,11 +170,11 @@
     pl.when(jnp.logical_not(has_low))(lambda: empty(0))
     pl.when(jnp.logical_not(has_high))(lambda: empty(1))
 
-    for h in range(PAIR):
-        for d in (1, 2, 3):
-            for t in (0, 1):
-                in_copy(t, h, d, False).wait_recv()
-                both_ways(lambda way: z_copy(way, t, h, d).start())
+    for d in (1, 2, 3):
+        relay(0, d)
+    send_inputs(1)
+    relay(1, 1)
+    acc[...] = jnp.zeros_like(acc)
 
     def chunk(h, c):
         q = qs[h, 2 * c:2 * c + 2].reshape(TILE, HEAD)
@@ -214,10 +220,18 @@
                 whole = (acc[h, 2 + part, t] + arrived[0, h, part, t].astype(F32)
                          + arrived[1, h, part, t].astype(F32))
                 final[t, h, 2 * part:2 * part + 2] = whole.astype(BF).reshape(2, ROWS, HEAD)
-        for t in (2, 3):
-            for d in (2, 3, 1):
-                out_copy(t, h, d).start()
-            out_own_copy(t, h).start()
+
+            @pl.when(side == part)
+            def _():
+                for t in (2, 3):
+                    out_copy(t, h, 1).start()
+                    out_own_copy(t, h).start()
+
+            @pl.when(side != part)
+            def _():
+                for t in (2, 3):
+                    out_copy(t, h, 2).start()
+                    out_copy(t, h, 3).start()
 
     def head(h, carry):
         for t in range(4):
@@ -237,14 +251,24 @@
                     remote(landing(t, h, block), landing(t, h, block), z_send.at[1 - way, t, h, d],
                            z_recv.at[1 - way, t, h, d], me + (-REACH if way == 0 else REACH)).wait_recv()
 
-        both_ways(window_arrival)
-        for i in range(6):
+        def turned(i):
             vt[i] = vw[h, 2 * i:2 * i + 2].reshape(TILE, HEAD).T
             kt[i] = kx[h, 2 * i:2 * i + 2, :, :HEAD].reshape(TILE, HEAD).T
+
+        turned(2)
+        turned(3)
+        both_ways(window_arrival)
+        for i in (0, 1, 4, 5):
+            turned(i)
         chunk(h, 0)
         stage[0, h, 0] = acc[h, 0].astype(BF)
         pl.when(has_low)(lambda: gz_copy(0, h, 0).start())
-        pl.when(h == 1)(lambda: finish(0))
+
+        @pl.when(h == 0)
+        def _():
+            relay(1, 2)
+            relay(1, 3)
+
         chunk(h, 1)
         stage[0, h, 1] = acc[h, 1].astype(BF)
         pl.when(has_low)(lambda: gz_copy(0, h, 1).start())
@@ -258,34 +282,47 @@
         return carry
 
     lax.fori_loop(0, PAIR, head, 0)
-    finish(1)
 
     for h in range(PAIR):
         for t in range(4):
             for d in (1, 2, 3):
                 in_copy(t, h, d, True).wait_send()
-                out_copy(t, h, d).wait_send()
-                out_arrival(t, h, d).wait_recv()
-            out_own_copy(t, h).wait()
 
         def sent(way):
             for t in range(2):
                 for d in range(4):
                     z_copy(way, t, h, d).wait_send()
-            for part in range(2):
-                gz_copy(way, h, part).wait_send()
 
         both_ways(sent)
+
+    finish(0)
+    finish(1)
+    for h in range(PAIR):
+        both_ways(lambda way: [gz_copy(way, h, part).wait_send() for part in range(2)] and None)
+        for t in range(4):
+            out_own_copy(t, h).wait()
+            for d in (1, 2, 3):
+                out_copy(t, h, d).wait_send()
+                out_arrival(t, h, d).wait_recv()
+
+
+def hand_over(*refs):
+    sources, results, sems = refs[:4], refs[4:8], refs[8]
+    copies = [pltpu.make_async_copy(sources[t], results[t], sems.at[t]) for t in range(4)]
+    for copy in copies:
+        copy.start()
+    for copy in copies:
+        copy.wait()
 
 
 def shards(slabs, query, key, value, out_grad, session):
     rows, features = query.shape
     dma = pltpu.SemaphoreType.DMA
     result = jax.ShapeDtypeStruct((rows, features), BF)
-    return pl.pallas_call(
+    done = pl.pallas_call(
         functools.partial(kernel, slabs),
         out_shape=(result,) * 4,
-        in_specs=[pl.BlockSpec(memory_space=pl.ANY)] * 4 + [pl.BlockSpec(memory_space=pltpu.VMEM)],
+        in_specs=[pl.BlockSpec(memory_space=pltpu.HBM)] * 4 + [pl.BlockSpec(memory_space=pltpu.VMEM)],
         out_specs=(pl.BlockSpec(memory_space=pl.ANY),) * 4,
         scratch_shapes=[
             pltpu.VMEM((PAIR, 3 * REACH, ROWS, 2 * HEAD), BF),
@@ -314,10 +351,18 @@
             dma((4, PAIR, 3)),
         ],
         compiler_params=pltpu.CompilerParams(
-            collective_id=0, has_side_effects=True, vmem_limit_bytes=40 * 1024 * 1024),
+            collective_id=0, has_side_effects=True, vmem_limit_bytes=62 * 1024 * 1024),
         cost_estimate=pl.CostEstimate(
             flops=2_000_000_000, bytes_accessed=2_100_000, transcendentals=1_300_000),
     )(query, key, value, out_grad, session.reshape(-1, ROWS))
+    return pl.pallas_call(
+        hand_over,
+        out_shape=(result,) * 4,
+        in_specs=[pl.BlockSpec(memory_space=pltpu.VMEM)] * 4,
+        out_specs=(pl.BlockSpec(memory_space=pltpu.HBM),) * 4,
+        scratch_shapes=[dma((4,))],
+        compiler_params=pltpu.CompilerParams(vmem_limit_bytes=62 * 1024 * 1024),
+    )(*done)
 
 
 def solution(mesh):

time: 47.5 us -> 41 us (0.86); the launches traced: 47.2 us -> 40.2 us
  local copies, waits for them, and re-layouts: 7.3 us -> 0 us
    unnamed x14 -> x0, local copies, waits for them, and re-layouts: 7.3 us -> none
    pallas_call x0 -> x1, Pallas kernels: none -> 2.18 us  [shards(): pl.pallas_call(hand_over, out_shape=(result,) * 4, in_specs=[pl.BlockSpec...]
    pallas_call x1, Pallas kernels: 39.3 us -> 37.4 us  [shards(): pl.pallas_call(functools.partial(kernel, slabs), out_shape=(result,) * 4,...]
where the time goes in v2:
time: 41 us; the launch traced here: 40.2 us
  Pallas kernels  39.6 us (97%)
  between operations  0.64 us (2%)
    pallas_call x1, Pallas kernels, shards(): pl.pallas_call(functools.partial(kernel, slabs), out_shape=(result,) * 4,...  37.4 us
    pallas_call x1, Pallas kernels, shards(): pl.pallas_call(hand_over, out_shape=(result,) * 4, in_specs=[pl.BlockSpec...  2.18 us

profile of v2, /device:TPU:17, one launch (start us, length us, event | category | flops | bytes accessed | tf_op | source)
XLA Modules:
  0.0 40.2 jit_solution(16714318233799764808)
XLA Ops:
  0.6 37.4 %shard_map.84 = (bf16[128,1024]{1,0:T(8,128)(2,1)}, bf16[128,1024]{1,0:T(8,128)(2,1)}, bf16[128,1024]{1,0:T(8,128)(2,1)}, bf16[128,1024]{1,0:T(8,128)(2,1)}) custom-call(bf16[128,1024]{1,0:T(8,128)(2,1)} %q_in.1, bf16[128,1024]{1,0:T(8,128)(2,1)} %k_in.1, bf16[128,1024]{1,0:T(8,128)(2,1)} %v_in.1, bf16[128,1024]{1,0:T(8,128)(2,1)} %g_in.1, s32[16,128]{1,0:T(8,128)} %bitcast.1), custom_call_target="tpu_custom_call" | custom-call | flops 2000000000 | bytes 2100000 | tf_op jit(solution)/shard_map/pallas_call | solution.py:322
  38.0 2.2 %shard_map.85 = (bf16[128,1024]{1,0:T(8,128)(2,1)}, bf16[128,1024]{1,0:T(8,128)(2,1)}, bf16[128,1024]{1,0:T(8,128)(2,1)}, bf16[128,1024]{1,0:T(8,128)(2,1)}) custom-call(bf16[128,1024]{1,0:T(8,128)(2,1)} %get-tuple-element.8.refs_0_, bf16[128,1024]{1,0:T(8,128)(2,1)} %get-tuple-element.9.refs_1_, bf16[128,1024]{1,0:T(8,128)(2,1)} %get-tuple-element.10.refs_2_, ...), custom_call_target="tpu_custom_call" | custom-call | tf_op jit(solution)/shard_map/pallas_call | solution.py:358

commit v3 on v2

--- a/solution.py
+++ b/solution.py
@@ -176,7 +176,7 @@
     relay(1, 1)
     acc[...] = jnp.zeros_like(acc)
 
-    def chunk(h, c):
+    def chunk(h, c, between=lambda: None):
         q = qs[h, 2 * c:2 * c + 2].reshape(TILE, HEAD)
         g = gs[h, 2 * c:2 * c + 2].reshape(TILE, HEAD)
         g_t = gt[c]
@@ -192,6 +192,7 @@
             e = jnp.exp((scores[i] - high) * SCALING)
             scores[i] = e
             total = total + jnp.sum(e, axis=0, keepdims=True)
+        between()
         share = 1.0 / total
         att = jnp.zeros((HEAD, TILE), F32)
         for i in range(5):
@@ -260,15 +261,16 @@
         both_ways(window_arrival)
         for i in (0, 1, 4, 5):
             turned(i)
-        chunk(h, 0)
+
+        def relay_next():
+            @pl.when(h == 0)
+            def _():
+                relay(1, 2)
+                relay(1, 3)
+
+        chunk(h, 0, relay_next)
         stage[0, h, 0] = acc[h, 0].astype(BF)
         pl.when(has_low)(lambda: gz_copy(0, h, 0).start())
-
-        @pl.when(h == 0)
-        def _():
-            relay(1, 2)
-            relay(1, 3)
-
         chunk(h, 1)
         stage[0, h, 1] = acc[h, 1].astype(BF)
         pl.when(has_low)(lambda: gz_copy(0, h, 1).start())
@@ -321,9 +323,9 @@
     result = jax.ShapeDtypeStruct((rows, features), BF)
     done = pl.pallas_call(
         functools.partial(kernel, slabs),
-        out_shape=(result,) * 4,
+        out_shape=(pltpu.VMEM((rows, features), BF),) * 4,
         in_specs=[pl.BlockSpec(memory_space=pltpu.HBM)] * 4 + [pl.BlockSpec(memory_space=pltpu.VMEM)],
-        out_specs=(pl.BlockSpec(memory_space=pl.ANY),) * 4,
+        out_specs=(pl.BlockSpec(memory_space=pltpu.VMEM),) * 4,
         scratch_shapes=[
             pltpu.VMEM((PAIR, 3 * REACH, ROWS, 2 * HEAD), BF),
             pltpu.VMEM((PAIR, 3 * REACH, ROWS, HEAD), BF),
@@ -358,10 +360,10 @@
     return pl.pallas_call(
         hand_over,
         out_shape=(result,) * 4,
-        in_specs=[pl.BlockSpec(memory_space=pltpu.VMEM)] * 4,
+        in_specs=[pl.BlockSpec(memory_space=pl.ANY)] * 4,
         out_specs=(pl.BlockSpec(memory_space=pltpu.HBM),) * 4,
         scratch_shapes=[dma((4,))],
-        compiler_params=pltpu.CompilerParams(vmem_limit_bytes=62 * 1024 * 1024),
+        compiler_params=pltpu.CompilerParams(vmem_limit_bytes=4 * 1024 * 1024),
     )(*done)
 
 

time: 41 us -> 36.5 us (0.89)
  the two profiles are of different devices: /device:TPU:17 before, /device:TPU:29 now
where the time goes in v3:
time: 36.5 us; the launch traced here: 36.3 us
  Pallas kernels  35.6 us (98%)
  between operations  0.64 us (2%)
    pallas_call x1, Pallas kernels, shards(): pl.pallas_call(functools.partial(kernel, slabs), out_shape=(pltpu.VMEM((r...  34.6 us
    pallas_call x1, Pallas kernels, shards(): pl.pallas_call(hand_over, out_shape=(result,) * 4, in_specs=[pl.BlockSpec...  1 us

profile of v3, /device:TPU:29, one launch (start us, length us, event | category | flops | bytes accessed | tf_op | source)
XLA Modules:
  0.0 36.3 jit_solution(6618253734741452027)
XLA Ops:
  0.6 34.6 %shard_map.84 = (bf16[128,1024]{1,0:T(8,128)(2,1)S(1)}, bf16[128,1024]{1,0:T(8,128)(2,1)S(1)}, bf16[128,1024]{1,0:T(8,128)(2,1)S(1)}, bf16[128,1024]{1,0:T(8,128)(2,1)S(1)}) custom-call(bf16[128,1024]{1,0:T(8,128)(2,1)} %q_in.1, bf16[128,1024]{1,0:T(8,128)(2,1)} %k_in.1, bf16[128,1024]{1,0:T(8,128)(2,1)} %v_in.1, bf16[128,1024]{1,0:T(8,128)(2,1)} %g_in.1, ...), custom_call_target="tpu_custom_call" | custom-call | flops 2000000000 | bytes 2100000 | tf_op jit(solution)/shard_map/pallas_call | solution.py:324
  35.3 1.0 %shard_map.85 = (bf16[128,1024]{1,0:T(8,128)(2,1)}, bf16[128,1024]{1,0:T(8,128)(2,1)}, bf16[128,1024]{1,0:T(8,128)(2,1)}, bf16[128,1024]{1,0:T(8,128)(2,1)}) custom-call(bf16[128,1024]{1,0:T(8,128)(2,1)S(1)} %get-tuple-element.8.refs_0_, bf16[128,1024]{1,0:T(8,128)(2,1)S(1)} %get-tuple-element.9.refs_1_, bf16[128,1024]{1,0:T(8,128)(2,1)S(1)} %get-tuple-element.10.refs_2_, ...), custom_call_target="tpu_custom_call" | custom-call | tf_op jit(solution)/shard_map/pallas_call | solution.py:360
